TPU v7x, 128 devices: a whole 4x4x4 slice. The times are simulated.
128 devices in a mesh: section: 4 (over x), group: 4 (over y_hi, core), head: 8 (over z, y_lo).
Axes of the slice: x: 4, y: 4 (y_hi: 2, y_lo: 2; y = y_hi * 2 + y_lo), z: 4, core: 2. Of those that a mesh axis runs over, the one named last changes fastest.
Arguments:
- queries: bfloat16 [4, 8, 128, 576], P('group', None, ('section', 'head')), may hold values from -84 to 84
- cache: bfloat16 [4, 8, 4096, 576], P('group', None, ('section', 'head')), may hold values from -6 to 6
- kept_length: int32 [4, 8], P('group'), may hold values from 1024 to 4096, as said below
- w_uv: bfloat16 [128, 512, 128], P(('section', 'head')), may hold values from -0.75 to 0.75
- w_out: bfloat16 [16384, 7168], P(('section', 'head')), may hold values from -0.09375 to 0.09375
- resid: bfloat16 [4, 8, 7168], P('group', 'section', 'head'), may hold values from -3 to 3
- picks: int32 [4, 8, 8], P('group', 'section'), may hold values from 0 to 15, all different within a row; in each aligned block of 2 rows (0 to 1, 2 to 3, ..., all dimensions but the last counted through in order) at most 2 rows name the same one
- pick_logits: float32 [4, 8, 8], P('group', 'section'), may hold values from -6 to 6
- w_gate: bfloat16 [16, 7168, 2048], P(('section', 'group'), 'head'), may hold values from -0.0625 to 0.0625
- w_up: bfloat16 [16, 7168, 2048], P(('section', 'group'), 'head'), may hold values from -0.0625 to 0.0625
- w_down: bfloat16 [16, 2048, 7168], P(('section', 'group'), None, 'head'), may hold values from -0.125 to 0.125
Outputs:
- out: bfloat16 [4, 8, 7168], P('group', 'section', 'head')
Inputs may be any that keep to these rules, and one draw needn't show every extreme that they name: Request j of group g keeps its first kept_length[g, j] positions; some request keeps all 4096. Each token picks 8 different experts; since each token's 8 picks differ, an expert receives at most 2 of the 2 tokens of one section index of a group.
All inputs are finite; a program needn't handle non-finite values.
Results may differ from a plain program's by a relative error of at most 0.012.
Values may be sent and summed in bfloat16 or wider, within the bound.
No kernel may reach another device: no remote copies, remote signals or barrier semaphores. Data moves between devices by JAX's collectives and lax.ppermute only.
A program may use at most 256 MiB of HBM per device.

v0:
```python
import jax
import jax.numpy as jnp
from jax import lax
from jax.sharding import PartitionSpec as P

LAT = 512
ROPE = 64
VDIM = 128
D = 7168


neg_fill = -1e30
norm_eps = 1e-06
route_scale = 2.5


def merged(shard, axis, combine):
    everything = jax.tree.map(lambda part: lax.all_gather(part, axis), shard)
    leading = jax.tree.map(lambda part: part[0], everything)

    def hop(k, so_far):
        return combine(so_far, jax.tree.map(lambda part: part[k], everything))

    return lax.fori_loop(1, lax.axis_size(axis), hop, leading)


def join_partial(earlier, later):
    max_a, sum_a, out_a = earlier
    max_b, sum_b, out_b = later
    larger = jnp.maximum(max_a, max_b)
    fac_a = jnp.exp(max_a - larger)
    fac_b = jnp.exp(max_b - larger)
    return (
        larger,
        fac_a * sum_a + fac_b * sum_b,
        fac_a[..., None] * out_a + fac_b[..., None] * out_b,
    )


def expert_rows(received, gate_mat, up_mat, down_mat):
    count_src, count_rows, row_width = received.shape
    flat_rows = received.reshape(count_src * count_rows, row_width)
    gate_part = jnp.dot(flat_rows, gate_mat, preferred_element_type=jnp.float32)
    up_part = jnp.dot(flat_rows, up_mat, preferred_element_type=jnp.float32)
    squares = jnp.sum(jnp.square(flat_rows.astype(jnp.float32)), axis=-1)
    gate_part, up_part, squares = lax.psum((gate_part, up_part, squares), "head")
    factor = lax.rsqrt(squares / D + norm_eps)[:, None]
    active = (jax.nn.silu(gate_part * factor) * (up_part * factor)).astype(jnp.bfloat16)
    result = jnp.dot(active, down_mat, preferred_element_type=jnp.float32).astype(jnp.bfloat16)
    return result.reshape(count_src, count_rows, down_mat.shape[1])


def local(
    queries, cache, kept_length, w_uv, w_out, resid, picks, pick_logits, w_gate, w_up, w_down
):
    n_section = lax.axis_size("section")
    n_group = lax.axis_size("group")
    n_head = lax.axis_size("head")
    shard_pos = lax.axis_index(("section", "head"))
    block_len = cache.shape[2]
    head_dev = queries.shape[2]
    req_group = queries.shape[1]
    score_scale = (VDIM + ROPE) ** (-0.5)
    all_queries = lax.all_gather(queries, ("section", "head"), axis=2, tiled=True)[0]
    page_rows = cache[0]
    scores = (
        jnp.einsum("jnd,jtd->jnt", all_queries, page_rows, preferred_element_type=jnp.float32)
        * score_scale
    )
    position = shard_pos * block_len + jnp.arange(block_len, dtype=jnp.int32)
    counted = (position[None, :] < kept_length[0][:, None])[:, None, :]
    masked = jnp.where(counted, scores, neg_fill)
    local_max = jnp.max(masked, axis=-1)
    weights = jnp.where(counted, jnp.exp(masked - local_max[..., None]), 0.0)
    local_sum = jnp.sum(weights, axis=-1)
    local_out = jnp.einsum(
        "jnt,jtl->jnl",
        weights.astype(jnp.bfloat16),
        page_rows[:, :, :LAT],
        preferred_element_type=jnp.float32,
    )
    merged_max, merged_sum, merged_out = merged(
        (local_max, local_sum, local_out), ("section", "head"), join_partial
    )
    head_start = shard_pos * head_dev
    own_sum = lax.dynamic_slice_in_dim(merged_sum, head_start, head_dev, 1)
    own_out = lax.dynamic_slice_in_dim(merged_out, head_start, head_dev, 1)
    latent = (own_out / own_sum[..., None]).astype(jnp.bfloat16)
    values = jnp.einsum("jnl,nlv->jnv", latent, w_uv, preferred_element_type=jnp.float32).astype(
        jnp.bfloat16
    )
    values = values.reshape(req_group, -1)
    rows_dev = resid.shape[1]
    width_dev = resid.shape[2]
    value_width = values.shape[1]
    by_section = values.reshape(n_section, rows_dev, value_width)
    by_head = w_out.reshape(value_width, n_head, width_dev)
    number = lax.axis_size(("section", "head")) * rows_dev // rows_dev
    blocks = jnp.arange(number, dtype=jnp.int32)
    chosen_rows = jnp.take(by_section, blocks // n_head, axis=0)
    chosen_cols = jnp.take(by_head, blocks % n_head, axis=1)
    term = jnp.einsum("brk,kbd->brd", chosen_rows, chosen_cols, preferred_element_type=jnp.float32)
    attended = lax.psum_scatter(
        term.reshape(lax.axis_size(("section", "head")) * rows_dev, width_dev),
        ("section", "head"),
        scatter_dimension=0,
        tiled=True,
    )
    hidden = (resid[0].astype(jnp.float32) + attended).astype(jnp.bfloat16)
    top_k = picks.shape[2]
    experts = n_section * n_group
    capacity = max(2, rows_dev * top_k * 3 // (2 * experts))
    chosen = picks[0].reshape(-1)
    onehot = (chosen[:, None] == jnp.arange(experts, dtype=jnp.int32)[None, :]).astype(jnp.int32)
    earlier = jnp.cumsum(onehot, axis=0) - onehot
    slot_index = chosen * capacity + jnp.sum(earlier * onehot, axis=1)
    slot_table = (
        slot_index[None, :] == jnp.arange(experts * capacity, dtype=jnp.int32)[:, None]
    ).astype(jnp.bfloat16)
    repeated = jnp.repeat(hidden, top_k, axis=0)
    outgoing = jnp.dot(slot_table, repeated, preferred_element_type=jnp.float32).astype(
        jnp.bfloat16
    )
    outgoing = outgoing.reshape(experts, capacity, width_dev)
    served = expert_rows(
        lax.all_to_all(outgoing, ("section", "group"), split_axis=0, concat_axis=0, tiled=True),
        w_gate[0],
        w_up[0],
        w_down[0],
    )
    returned_rows = lax.all_to_all(
        served, ("section", "group"), split_axis=0, concat_axis=0, tiled=True
    )
    per_pick = jnp.dot(
        slot_table.T,
        returned_rows.reshape(experts * capacity, width_dev),
        preferred_element_type=jnp.float32,
    )
    per_pick = per_pick.reshape(rows_dev, top_k, width_dev)
    affinity = jax.nn.sigmoid(pick_logits[0])
    pick_share = route_scale * affinity / jnp.sum(affinity, axis=-1, keepdims=True)
    mixture = jnp.sum(pick_share[..., None] * per_pick, axis=1)
    return (hidden.astype(jnp.float32) + mixture).astype(jnp.bfloat16)[None]


def solution(mesh):
    return jax.shard_map(
        local,
        mesh=mesh,
        in_specs=(
            P("group", None, ("section", "head"), None),
            P("group", None, ("section", "head"), None),
            P("group", None),
            P(("section", "head"), None, None),
            P(("section", "head"), None),
            P("group", "section", "head"),
            P("group", "section", None),
            P("group", "section", None),
            P(("section", "group"), "head", None),
            P(("section", "group"), "head", None),
            P(("section", "group"), None, "head"),
        ),
        out_specs=P("group", "section", "head"),
        check_vma=False,
    )
```

profile of v0, /device:TPU:1, one launch (start us, length us, event | category | flops | bytes accessed | tf_op | source)
XLA Modules:
  0.0 2082.4 jit_solution(10861690201370815967)
XLA Ops:
  8.1 2.4 copy.33
  11.3 131.5 %all-gather.6.cloned.1.call-done = bf16[1,8,128,576]{3,1,0,2:T(8,128)(2,1)} async-done(((bf16[1,8,4,576]{3,1,0,2:T(8,128)(2,1)}), bf16[1,8,128,576]{3,1,0,2:T(8,128)(2,1)}) %all-gather.6.cloned.1.call-update) | async-done | bytes 1179664 | tf_op jit(solution)/shard_map/all_gather | solution.py:64
  142.8 2.2 copy.32
  145.7 3.3 fusion.22
  149.0 10.4 copy.38
  159.4 11.4 copy.39
  171.0 14.6 gather_fusion.1
  185.9 96.5 %all-gather.1 = f32[256,128]{1,0:T(8,128)S(1)} all-gather(f32[8,128]{1,0:T(8,128)S(1)} %fusion.25), channel_id=3, replica_groups=mesh['section'=4,'group'=4,'head'=8] {'section','head'}, dimensions={0}, use_global_device_ids=true | all-gather | bytes 135168 | tf_op jit(solution)/shard_map/all_gather | solution.py:18
  282.4 70.8 %all-gather = f32[256,128]{1,0:T(8,128)S(1)} all-gather(f32[8,128]{1,0:T(8,128)S(1)} %get-tuple-element.206), channel_id=2, replica_groups=mesh['section'=4,'group'=4,'head'=8] {'section','head'}, dimensions={0}, use_global_device_ids=true | all-gather | bytes 135168 | tf_op jit(solution)/shard_map/all_gather | solution.py:18
  353.2 1228.7 %all-gather.8.cloned.1.call-done = f32[256,128,512]{2,1,0:T(8,128)} async-done(((f32[8,128,512]{2,1,0:T(8,128)}), f32[256,128,512]{2,1,0:T(8,128)}) %all-gather.8.cloned.1.call-update) | async-done | bytes 67108880 | tf_op jit(solution)/shard_map/all_gather | solution.py:18
  1583.7 68.6 %while.19 = (s32[]{:T(128)}, f32[8,128]{1,0:T(8,128)S(1)}, f32[8,128]{1,0:T(8,128)S(1)}, f32[8,128,512]{2,1,0:T(8,128)S(1)}, f32[32,8,128]{2,1,0:T(8,128)S(1)}, ...) while((s32[]{:T(128)}, f32[8,128]{1,0:T(8,128)S(1)}, ...), condition=%wide.region_3.4_spmd, body=%wide.region_2.3_spmd.sunk | while | flops 1579013 | bytes 6332567 | solution.py:24
  1583.8 2.2 fusion.59
  1586.0 2.2 fusion.59
  1588.2 2.2 fusion.59
  1590.4 2.2 fusion.59
  1594.8 2.2 fusion.59
  1597.0 2.2 fusion.59
  1599.2 2.2 fusion.59
  1601.5 2.2 fusion.59
  1603.7 2.2 fusion.59
  1605.9 2.2 fusion.59
  1608.1 2.2 fusion.59
  1610.3 2.2 fusion.59
  1612.5 2.2 fusion.59
  1614.7 2.2 fusion.59
  1616.9 2.2 fusion.59
  1619.2 2.2 fusion.59
  1621.4 2.2 fusion.59
  1623.6 2.2 fusion.59
  1625.8 2.2 fusion.59
  1628.0 2.2 fusion.59
  1630.2 2.2 fusion.59
  1632.4 2.2 fusion.59
  1636.8 2.2 fusion.59
  1639.1 2.2 fusion.59
  1641.3 2.2 fusion.59
  1643.5 2.2 fusion.59
  1645.7 2.2 fusion.59
  1653.4 11.8 fusion.3
  1667.6 277.9 %all-reduce.5.cloned.1.call-done = f32[64,896]{1,0:T(8,128)} async-done(((f32[64,896]{1,0:T(8,128)}), f32[64,896]{1,0:T(8,128)}) %all-reduce.5.cloned.1.call-update) | async-done | bytes 229392
  1947.1 25.2 %all-to-all-start = ((bf16[16,2,896]{2,1,0:T(2,128)(2,1)}), bf16[16,2,896]{2,1,0:T(2,128)(2,1)S(1)}, u32[]{:S(2)}, u32[]{:S(2)}) async-start(bf16[16,2,896]{2,1,0:T(2,128)(2,1)} %reshape.202), calls=%async_computation | async-start | bytes 114688 | tf_op jit(solution)/shard_map/all_to_all | solution.py:126
  1972.4 7.3 all-to-all-done
  1979.8 3.6 fusion.10
  1985.3 13.8 psum.22
  1999.0 53.3 %all-reduce.7.cloned.1.call-done = (f32[32,2048]{1,0:T(8,128)}, f32[32,2048]{1,0:T(8,128)}) async-done(((f32[32,2048]{1,0:T(8,128)}, f32[32,2048]{1,0:T(8,128)}), (f32[32,2048]{1,0:T(8,128)}, f32[32,2048]{1,0:T(8,128)})) %all-reduce.7.cloned.1.call-update) | async-done | bytes 524304 | tf_op jit(solution)/shard_map/psum | solution.py:46
  2052.4 2.9 fusion.17
  2056.0 11.7 all-to-all-start.1
  2067.8 7.3 all-to-all-done.1
  (98 shorter events, 22.3 us)
Async XLA Ops:
  6.5 1645.9 %copy-start = (bf16[4,512,128]{2,1,0:T(8,128)(2,1)S(1)}, bf16[4,512,128]{2,1,0:T(8,128)(2,1)}, u32[]{:S(2)}) copy-start(bf16[4,512,128]{2,1,0:T(8,128)(2,1)} %param.16) | copy-start | bytes 1572868
  6.5 138.5 %copy-start.1 = (bf16[1,8,128,576]{2,3,1,0:T(8,128)(2,1)S(1)}, bf16[1,8,128,576]{2,3,1,0:T(8,128)(2,1)}, u32[]{:S(2)}) copy-start(bf16[1,8,128,576]{2,3,1,0:T(8,128)(2,1)} %param.14) | copy-start | bytes 3538948
  6.5 136.3 %all-gather.6.cloned.1.call-start = ((), (), s32[]{:S(2)}) async-start(), calls=%async_computation.2 | async-start | bytes 1351680 | tf_op jit(solution)/shard_map/all_gather | solution.py:64
  8.1 1573.8 %all-gather.8.cloned.1.call-start = ((), (), s32[]{:S(2)}) async-start(), calls=%async_computation.3 | async-start | bytes 69206016 | tf_op jit(solution)/shard_map/all_gather | solution.py:18
  148.9 1796.6 %all-reduce.5.cloned.1.call-start = ((), (), s32[]{:S(2)}) async-start(), calls=%async_computation.4 | async-start | bytes 458752
  159.4 11.4 copy-start.4
  1653.4 13.0 copy-start.6
  1653.4 292.2 %copy-start.3 = (bf16[1,2,896]{2,1,0:T(2,128)(2,1)S(1)}, bf16[1,2,896]{2,1,0:T(2,128)(2,1)}, u32[]{:S(2)}) copy-start(bf16[1,2,896]{2,1,0:T(2,128)(2,1)} %param.18) | copy-start | bytes 10756
  1947.1 32.6 %all-to-all-start = ((bf16[16,2,896]{2,1,0:T(2,128)(2,1)}), bf16[16,2,896]{2,1,0:T(2,128)(2,1)S(1)}, u32[]{:S(2)}, u32[]{:S(2)}) async-start(bf16[16,2,896]{2,1,0:T(2,128)(2,1)} %reshape.202), calls=%async_computation | async-start | bytes 114688 | tf_op jit(solution)/shard_map/all_to_all | solution.py:126
  1972.4 80.0 %all-reduce.7.cloned.1.call-start = ((), (), s32[]{:S(2)}) async-start(), calls=%async_computation.5 | async-start | bytes 1048576 | tf_op jit(solution)/shard_map/psum | solution.py:46
  1979.8 3.7 copy-start.2
  1979.8 5.1 copy-start.5
  2056.0 19.1 all-to-all-start.1
Sparse Core Ops, SparseCore 0:
  9.0 133.7 all-gather.5
  149.1 1432.7 all-gather.7
  1666.2 279.3 all-reduce.4
  1985.0 67.2 all-reduce.6
where the time goes:
time: 2080 us
  waiting for transfers between devices  1710 us (82%)
  blocking collectives  181 us (9%)
  other arithmetic  70.6 us (3%)
  local copies, waits for them, and re-layouts  48.3 us (2%)
  starting transfers between devices  37.1 us (2%)
  matrix products  24.3 us (1%)
    all_gather x1, waiting for transfers between devices, merged(): everything = jax.tree.map(lambda part: lax.all_gather(part, axis), shard)  1230 us
    unnamed x5, waiting for transfers between devices  278 us
    all_gather x2, blocking collectives, merged(): everything = jax.tree.map(lambda part: lax.all_gather(part, axis), shard)  167 us
    all_gather x1, waiting for transfers between devices, local(): lax.all_gather(queries, ('section', 'head'), axis=2, tiled=True)[0]  132 us
    add x31, other arithmetic, join_partial(): fac_a[..., None] * out_a + fac_b[..., None] * out_b  67 us
    psum x1, waiting for transfers between devices, expert_rows(): lax.psum((gate_part, up_part, squares), 'head')  53.3 us
  transfers between devices with their start and end apart: 6, of which 6 were waited for; matrix products, arithmetic and copies ran while one was open for 2% of the time, Pallas kernels for 0%

commit v1 on v0

v1 whole, which is shorter than its diff:
```python
import jax
import jax.numpy as jnp
from jax import lax
from jax.sharding import PartitionSpec as P

LAT = 512
ROPE = 64
VDIM = 128
D = 7168

neg_fill = -1e30
norm_eps = 1e-06
route_scale = 2.5
f32 = jnp.float32
bf16 = jnp.bfloat16


def exchange(x, axes):
    return lax.all_to_all(x, axes, split_axis=0, concat_axis=0, tiled=True)


def parts_of(x):
    high = lax.reduce_precision(x, 8, 7)
    rest = x - high
    middle = lax.reduce_precision(rest, 8, 7)
    return high.astype(bf16), middle.astype(bf16), (rest - middle).astype(bf16)


def local(
    queries, cache, kept_length, w_uv, w_out, resid, picks, pick_logits, w_gate, w_up, w_down
):
    n_section = lax.axis_size("section")
    n_group = lax.axis_size("group")
    n_head = lax.axis_size("head")
    n_shard = n_section * n_head
    n_expert = n_section * n_group
    section = lax.axis_index("section")
    group = lax.axis_index("group")
    head = lax.axis_index("head")
    reqs, heads_dev, width = queries.shape[1:]
    block_len = cache.shape[2]
    rows_dev, width_dev = resid.shape[1:]

    spread = jnp.broadcast_to(queries[0][None], (n_section, reqs, heads_dev, width))
    q_all = exchange(spread.reshape(n_shard, heads_dev, width), ("section", "head"))
    q_all = q_all.reshape(n_shard * heads_dev, width)
    pages = exchange(jnp.swapaxes(cache[0], 1, 2), "head")

    scores = jnp.einsum("nd,bdt->nbt", q_all, pages, preferred_element_type=f32) * (
        (VDIM + ROPE) ** -0.5
    )
    position = (section * n_head * block_len) + jnp.arange(n_head * block_len, dtype=jnp.int32)
    length = lax.dynamic_index_in_dim(kept_length[0], head, 0, keepdims=False)
    counted = (position < length).reshape(1, n_head, block_len)
    masked = jnp.where(counted, scores, neg_fill)
    top = jnp.max(masked, axis=(1, 2), keepdims=True)
    weights = jnp.where(counted, jnp.exp(masked - top), 0.0)
    total = jnp.sum(weights, axis=(1, 2))
    part_out = jnp.einsum(
        "nbt,blt->nl", weights.astype(bf16), pages[:, :LAT], preferred_element_type=f32
    )
    any_kept = total > 0
    safe = jnp.where(any_kept, total, 1.0)
    part_out = (part_out / safe[:, None]).astype(bf16)
    level = jnp.where(any_kept, top[:, 0, 0] + jnp.log(safe), neg_fill)
    extra = jnp.stack(parts_of(level), axis=-1)
    extra = jnp.pad(extra, ((0, 0), (0, 125)))
    sent = jnp.concatenate([part_out, extra], axis=1).reshape(n_shard, heads_dev, LAT + 128)
    got = exchange(sent, ("section", "head")).reshape(n_section, reqs, heads_dev, LAT + 128)
    levels = jnp.sum(got[..., LAT : LAT + 3].astype(f32), axis=-1)
    share = jnp.exp(levels - jnp.max(levels, axis=0))
    share = share / jnp.sum(share, axis=0)
    latent = jnp.sum(share[..., None] * got[..., :LAT].astype(f32), axis=0).astype(bf16)

    values = jnp.einsum("jnl,nlv->jnv", latent, w_uv, preferred_element_type=f32).astype(bf16)
    values = values.reshape(reqs, heads_dev * VDIM)
    term = jnp.dot(values, w_out, preferred_element_type=f32).astype(bf16)
    term = jnp.swapaxes(term.reshape(reqs, n_head, width_dev), 0, 1)
    term = jnp.sum(exchange(term, "head").astype(f32), axis=0)
    own = (jnp.arange(reqs) // rows_dev == section)[:, None]
    term = term + jnp.where(own, jnp.tile(resid[0].astype(f32), (n_section, 1)), 0.0)
    term = jnp.broadcast_to(term.astype(bf16)[None], (n_expert, reqs, width_dev))
    terms = exchange(term, ("section", "group")).reshape(n_section, n_group, reqs, width_dev)
    hidden = jnp.sum(terms.astype(f32), axis=0).astype(bf16)
    rows = hidden.reshape(n_group * reqs, width_dev)

    gate = jnp.dot(rows, w_gate[0], preferred_element_type=f32).astype(bf16)
    up = jnp.dot(rows, w_up[0], preferred_element_type=f32).astype(bf16)
    squares = jnp.sum(jnp.square(rows.astype(f32)), axis=-1)
    extra = jnp.pad(jnp.stack(parts_of(squares), axis=-1), ((0, 0), (0, 125)))
    count = rows.shape[0]
    ff_dev = gate.shape[1] // n_head
    both = jnp.concatenate(
        [
            gate.reshape(count, n_head, ff_dev),
            up.reshape(count, n_head, ff_dev),
            jnp.broadcast_to(extra[:, None], (count, n_head, 128)),
        ],
        axis=-1,
    )
    both = jnp.sum(exchange(jnp.swapaxes(both, 0, 1), "head").astype(f32), axis=0)
    squares = jnp.sum(both[:, 2 * ff_dev : 2 * ff_dev + 3], axis=-1, keepdims=True)
    factor = lax.rsqrt(squares / D + norm_eps)
    act = jax.nn.silu(both[:, :ff_dev] * factor) * (both[:, ff_dev : 2 * ff_dev] * factor)
    act = jnp.broadcast_to(act.astype(bf16)[None], (n_head, count, ff_dev))
    act = jnp.swapaxes(exchange(act, "head"), 0, 1).reshape(count, n_head * ff_dev)
    served = jnp.dot(act, w_down[0], preferred_element_type=f32).astype(bf16)
    served = served.reshape(n_group, n_section, rows_dev, width_dev)
    served = jnp.swapaxes(served, 0, 1).reshape(n_expert, rows_dev, width_dev)
    back = exchange(served, ("section", "group"))

    affinity = jax.nn.sigmoid(pick_logits[0])
    pick_share = route_scale * affinity / jnp.sum(affinity, axis=-1, keepdims=True)
    named = picks[0][..., None] == jnp.arange(n_expert, dtype=jnp.int32)
    weight = jnp.sum(jnp.where(named, pick_share[..., None], 0.0), axis=1)
    mixture = jnp.sum(weight.T[..., None] * back.astype(f32), axis=0)
    mine = lax.dynamic_slice(
        rows, (group * reqs + section * rows_dev, 0), (rows_dev, width_dev)
    )
    return (mine.astype(f32) + mixture).astype(bf16)[None]


def solution(mesh):
    return jax.shard_map(
        local,
        mesh=mesh,
        in_specs=(
            P("group", None, ("section", "head"), None),
            P("group", None, ("section", "head"), None),
            P("group", None),
            P(("section", "head"), None, None),
            P(("section", "head"), None),
            P("group", "section", "head"),
            P("group", "section", None),
            P("group", "section", None),
            P(("section", "group"), "head", None),
            P(("section", "group"), "head", None),
            P(("section", "group"), None, "head"),
        ),
        out_specs=P("group", "section", "head"),
        check_vma=False,
    )
```

time: 2080 us -> 127 us (0.06)
  waiting for transfers between devices: 1710 us -> 46 us
  blocking collectives: 181 us -> 33.9 us
  other arithmetic: 70.6 us -> 3.49 us
  local copies, waits for them, and re-layouts: 48.3 us -> 4.89 us
    all_gather x2 -> x0, waiting for transfers between devices: 1360 us -> none  [the longest x1 1230 us: merged(): everything = jax.tree.map(lambda part: lax.all_gather(part, axis), shard)]
    unnamed x5 -> x0, waiting for transfers between devices: 278 us -> none
    all_gather x2 -> x0, blocking collectives: 167 us -> none  [merged(): everything = jax.tree.map(lambda part: lax.all_gather(part, axis), shard)]
    add x65 -> x0, other arithmetic: 67.5 us -> none  [the longest x31 67 us: join_partial(): fac_a[..., None] * out_a + fac_b[..., None] * out_b]
    psum x1 -> x0, waiting for transfers between devices: 53.3 us -> none  [expert_rows(): lax.psum((gate_part, up_part, squares), 'head')]
    all_to_all x0 -> x2, blocking collectives: none -> 33.9 us  [exchange(): return lax.all_to_all(x, axes, split_axis=0, concat_axis=0, tiled=True)]
    all_to_all x2 -> x6, waiting for transfers between devices: 14.6 us -> 46 us  [exchange(): return lax.all_to_all(x, axes, split_axis=0, concat_axis=0, tiled=True)]
where the time goes in v1:
time: 127 us; the launch traced here: 126 us
  waiting for transfers between devices  46 us (36%)
  blocking collectives  33.9 us (27%)
  starting transfers between devices  24.7 us (19%)
  matrix products  12.7 us (10%)
  local copies, waits for them, and re-layouts  4.89 us (4%)
  other arithmetic  3.49 us (3%)
    all_to_all x6, waiting for transfers between devices, exchange(): return lax.all_to_all(x, axes, split_axis=0, concat_axis=0, tiled=True)  46 us
    all_to_all x2, blocking collectives, exchange(): return lax.all_to_all(x, axes, split_axis=0, concat_axis=0, tiled=True)  33.9 us
    all_to_all x6, starting transfers between devices, exchange(): return lax.all_to_all(x, axes, split_axis=0, concat_axis=0, tiled=True)  24.7 us
    dot_general x1, matrix products, local(): term = jnp.dot(values, w_out, preferred_element_type=f32).astype(bf16)  4.9 us
    dot_general x1, matrix products, local(): gate = jnp.dot(rows, w_gate[0], preferred_element_type=f32).astype(bf16)  2.92 us
    dot_general x1, matrix products, local(): served = jnp.dot(act, w_down[0], preferred_element_type=f32).astype(bf16)  2.7 us
  transfers between devices with their start and end apart: 6, of which 6 were waited for; matrix products, arithmetic and copies ran while one was open for 2% of the time, Pallas kernels for 0%

profile of v1, /device:TPU:1, one launch (start us, length us, event | category | flops | bytes accessed | tf_op | source)
XLA Modules:
  0.0 126.0 jit_solution(3257003622155249799)
XLA Ops:
  0.0 0.9 broadcast_in_dim.92
  0.9 17.1 %all_to_all.40 = bf16[32,4,576]{2,1,0:T(4,128)(2,1)S(1)} all-to-all(bf16[32,4,576]{2,1,0:T(4,128)(2,1)S(1)} %bitcast.87), channel_id=1, replica_groups=mesh['section'=4,'group'=4,'head'=8] {'section','head'}, dimensions={0} | all-to-all | bytes 294912 | tf_op jit(solution)/shard_map/all_to_all | solution.py:19
  17.9 3.6 %all-to-all-start.1 = ((bf16[8,576,128]{2,1,0:T(8,128)(2,1)}), bf16[8,576,128]{2,1,0:T(8,128)(2,1)S(1)}, u32[]{:S(2)}, u32[]{:S(2)}) async-start(bf16[8,576,128]{2,1,0:T(8,128)(2,1)} %bitcast.82), calls=%async_computation.1 | async-start | bytes 2359296 | tf_op jit(solution)/shard_map/all_to_all | solution.py:19
  21.5 0.0 copy-start.2
  21.5 1.2 constant_dynamic-slice_fusion
  22.8 0.7 add_compare_fusion
  23.4 0.1 reshape.261
  23.5 13.0 %all-to-all-done.1 = bf16[8,576,128]{2,1,0:T(8,128)(2,1)S(1)} async-done(((bf16[8,576,128]{2,1,0:T(8,128)(2,1)}), bf16[8,576,128]{2,1,0:T(8,128)(2,1)S(1)}, u32[]{:S(2)}, u32[]{:S(2)}) %all-to-all-start.1) | async-done | bytes 1179680 | tf_op jit(solution)/shard_map/all_to_all | solution.py:19
  36.5 0.7 fusion.45
  37.2 0.2 fusion.20
  37.5 0.1 copy.37
  37.7 0.7 fusion.17
  38.4 0.7 reshape.262
  39.1 5.3 %all-to-all-start.2 = ((bf16[32,4,640]{2,1,0:T(4,128)(2,1)}), bf16[32,4,640]{2,1,0:T(4,128)(2,1)S(1)}, u32[]{:S(2)}, u32[]{:S(2)}) async-start(bf16[32,4,640]{2,1,0:T(4,128)(2,1)} %reshape.262), calls=%async_computation.2 | async-start | bytes 327680 | tf_op jit(solution)/shard_map/all_to_all | solution.py:19
  44.5 7.5 %all-to-all-done.2 = bf16[32,4,640]{2,1,0:T(4,128)(2,1)S(1)} async-done(((bf16[32,4,640]{2,1,0:T(4,128)(2,1)}), bf16[32,4,640]{2,1,0:T(4,128)(2,1)S(1)}, u32[]{:S(2)}, u32[]{:S(2)}) %all-to-all-start.2) | async-done | bytes 163872 | tf_op jit(solution)/shard_map/all_to_all | solution.py:19
  52.0 0.1 convert_reduce_fusion.2
  52.1 0.2 multiply_reduce_fusion
  52.3 4.9 %convolution_convert_fusion = bf16[8,7168]{1,0:T(8,128)(2,1)} fusion(bf16[512,7168]{1,0:T(8,128)(2,1)} %param.15, bf16[4,512,128]{2,1,0:T(8,128)(2,1)S(1)} %copy-done, bf16[8,4,512]{2,1,0:T(4,128)(2,1)S(1)} %multiply_reduce_fusion), kind=kOutput, calls=%fused_computation | convolution fusion | flops 62976000 | bytes 8011776 | tf_op jit(solution)/shard_map/dot_general | solution.py:77
  57.2 3.4 %all-to-all-start.3 = ((bf16[8,8,896]{2,1,0:T(8,128)(2,1)}), bf16[8,8,896]{2,1,0:T(8,128)(2,1)S(1)}, u32[]{:S(2)}, u32[]{:S(2)}) async-start(bf16[8,8,896]{2,1,0:T(8,128)(2,1)} %bitcast.14), calls=%async_computation.3 | async-start | bytes 229376 | tf_op jit(solution)/shard_map/all_to_all | solution.py:19
  60.6 5.4 %all-to-all-done.3 = bf16[8,8,896]{2,1,0:T(8,128)(2,1)S(1)} async-done(((bf16[8,8,896]{2,1,0:T(8,128)(2,1)}), bf16[8,8,896]{2,1,0:T(8,128)(2,1)S(1)}, u32[]{:S(2)}, u32[]{:S(2)}) %all-to-all-start.3) | async-done | bytes 114720 | tf_op jit(solution)/shard_map/all_to_all | solution.py:19
  66.0 0.1 add_convert_fusion
  66.1 16.8 %all_to_all.41 = bf16[16,8,896]{2,1,0:T(8,128)(2,1)S(1)} all-to-all(bf16[16,8,896]{2,1,0:T(8,128)(2,1)S(1)} %broadcast_in_dim.100), channel_id=1, replica_groups=mesh['section'=4,'group'=4,'head'=8] {'section','group'}, dimensions={0} | all-to-all | bytes 458752 | tf_op jit(solution)/shard_map/all_to_all | solution.py:19
  83.0 0.0 copy-start.1
  83.0 0.1 multiply_reduce_fusion.2
  83.1 2.9 %fusion.6 = bf16[32,2048]{1,0:T(8,128)(2,1)S(1)} fusion(bf16[1,896,2048]{2,1,0:T(8,128)(2,1)} %param.19, bf16[4,8,896]{2,1,0:T(8,128)(2,1)S(1)} %reduce_sum.121), kind=kOutput, calls=%fused_computation.7 | convolution fusion | flops 117506048 | bytes 3858432 | tf_op jit(solution)/shard_map/dot_general | solution.py:87
  86.0 0.1 copy-done.1
  86.1 0.7 fusion.9
  86.9 0.1 reduce_sum.125
  87.0 0.0 copy-start.3
  87.0 0.1 copy.48
  87.1 0.7 maximum_bitcast_fusion
  87.9 3.4 %all-to-all-start.5 = ((bf16[8,32,640]{2,1,0:T(8,128)(2,1)}), bf16[8,32,640]{2,1,0:T(8,128)(2,1)S(1)}, u32[]{:S(2)}, u32[]{:S(2)}) async-start(bf16[8,32,640]{2,1,0:T(8,128)(2,1)} %maximum_bitcast_fusion), calls=%async_computation.5 | async-start | bytes 655360 | tf_op jit(solution)/shard_map/all_to_all | solution.py:19
  91.3 0.1 fusion.44
  91.5 7.5 %all-to-all-done.5 = bf16[8,32,640]{2,1,0:T(8,128)(2,1)S(1)} async-done(((bf16[8,32,640]{2,1,0:T(8,128)(2,1)}), bf16[8,32,640]{2,1,0:T(8,128)(2,1)S(1)}, u32[]{:S(2)}, u32[]{:S(2)}) %all-to-all-start.5) | async-done | bytes 327712 | tf_op jit(solution)/shard_map/all_to_all | solution.py:19
  99.0 0.1 slice_reduce_fusion
  99.1 0.1 fusion.30
  99.2 0.6 broadcast_in_dim.104
  99.9 3.4 %all-to-all-start.6 = ((bf16[8,32,256]{2,1,0:T(8,128)(2,1)}), bf16[8,32,256]{2,1,0:T(8,128)(2,1)S(1)}, u32[]{:S(2)}, u32[]{:S(2)}) async-start(bf16[8,32,256]{2,1,0:T(8,128)(2,1)} %broadcast_in_dim.104), calls=%async_computation.6 | async-start | bytes 262144 | tf_op jit(solution)/shard_map/all_to_all | solution.py:19
  103.3 0.1 bitcast_divide_fusion
  103.3 5.4 %all-to-all-done.6 = bf16[8,32,256]{2,1,0:T(8,128)(2,1)S(1)} async-done(((bf16[8,32,256]{2,1,0:T(8,128)(2,1)}), bf16[8,32,256]{2,1,0:T(8,128)(2,1)S(1)}, u32[]{:S(2)}, u32[]{:S(2)}) %all-to-all-start.6) | async-done | bytes 131104 | tf_op jit(solution)/shard_map/all_to_all | solution.py:19
  108.7 2.7 %fusion.13 = bf16[32,896]{1,0:T(8,128)(2,1)S(1)} fusion(bf16[32,2048]{1,0:T(8,128)(2,1)S(1)} %bitcast.89, bf16[1,2048,896]{2,1,0:T(8,128)(2,1)} %param.21), kind=kOutput, calls=%fused_computation.12 | convolution fusion | flops 117469184 | bytes 3858432 | tf_op jit(solution)/shard_map/dot_general | solution.py:107
  111.5 0.7 copy.44
  112.2 5.7 %all-to-all-start.7 = ((bf16[16,2,896]{2,1,0:T(2,128)(2,1)}), bf16[16,2,896]{2,1,0:T(2,128)(2,1)S(1)}, u32[]{:S(2)}, u32[]{:S(2)}) async-start(bf16[16,2,896]{2,1,0:T(2,128)(2,1)} %bitcast.27), calls=%async_computation.7 | async-start | bytes 114688 | tf_op jit(solution)/shard_map/all_to_all | solution.py:19
  117.8 0.1 select_reduce_fusion
  117.9 0.1 copy.39
  118.0 7.2 %all-to-all-done.7 = bf16[16,2,896]{2,1,0:T(2,128)(2,1)S(1)} async-done(((bf16[16,2,896]{2,1,0:T(2,128)(2,1)}), bf16[16,2,896]{2,1,0:T(2,128)(2,1)S(1)}, u32[]{:S(2)}, u32[]{:S(2)}) %all-to-all-start.7) | async-done | bytes 57376 | tf_op jit(solution)/shard_map/all_to_all | solution.py:19
  125.2 0.1 multiply_reduce_fusion.1
  125.4 0.6 fusion.35
  (30 shorter events, 0.4 us)
Async XLA Ops:
  0.0 52.3 %copy-start = (bf16[4,512,128]{2,1,0:T(8,128)(2,1)S(1)}, bf16[4,512,128]{2,1,0:T(8,128)(2,1)}, u32[]{:S(2)}) copy-start(bf16[4,512,128]{2,1,0:T(8,128)(2,1)} %param.14) | copy-start | bytes 1572868
  17.9 18.6 %all-to-all-start.1 = ((bf16[8,576,128]{2,1,0:T(8,128)(2,1)}), bf16[8,576,128]{2,1,0:T(8,128)(2,1)S(1)}, u32[]{:S(2)}, u32[]{:S(2)}) async-start(bf16[8,576,128]{2,1,0:T(8,128)(2,1)} %bitcast.82), calls=%async_computation.1 | async-start | bytes 2359296 | tf_op jit(solution)/shard_map/all_to_all | solution.py:19
  21.5 22.9 %copy-start.2 = (bf16[1,2,896]{2,1,0:T(2,128)(2,1)S(1)}, bf16[1,2,896]{2,1,0:T(2,128)(2,1)}, u32[]{:S(2)}) copy-start(bf16[1,2,896]{2,1,0:T(2,128)(2,1)} %param.16) | copy-start | bytes 10756
  39.1 12.8 %all-to-all-start.2 = ((bf16[32,4,640]{2,1,0:T(4,128)(2,1)}), bf16[32,4,640]{2,1,0:T(4,128)(2,1)S(1)}, u32[]{:S(2)}, u32[]{:S(2)}) async-start(bf16[32,4,640]{2,1,0:T(4,128)(2,1)} %reshape.262), calls=%async_computation.2 | async-start | bytes 327680 | tf_op jit(solution)/shard_map/all_to_all | solution.py:19
  57.2 8.8 %all-to-all-start.3 = ((bf16[8,8,896]{2,1,0:T(8,128)(2,1)}), bf16[8,8,896]{2,1,0:T(8,128)(2,1)S(1)}, u32[]{:S(2)}, u32[]{:S(2)}) async-start(bf16[8,8,896]{2,1,0:T(8,128)(2,1)} %bitcast.14), calls=%async_computation.3 | async-start | bytes 229376 | tf_op jit(solution)/shard_map/all_to_all | solution.py:19
  83.0 3.1 %copy-start.1 = (bf16[1,896,2048]{2,1,0:T(8,128)(2,1)S(1)}, bf16[1,896,2048]{2,1,0:T(8,128)(2,1)}, u32[]{:S(2)}) copy-start(bf16[1,896,2048]{2,1,0:T(8,128)(2,1)} %param.20) | copy-start | bytes 11010052
  86.1 5.2 %copy-start.4 = (f32[1,2,8]{2,1,0:T(2,128)S(1)}, f32[1,2,8]{2,1,0:T(2,128)}, u32[]{:S(2)}) copy-start(f32[1,2,8]{2,1,0:T(2,128)} %param.18) | copy-start | bytes 196
  87.0 30.8 %copy-start.3 = (s32[1,2,8]{2,1,0:T(2,128)S(1)}, s32[1,2,8]{2,1,0:T(2,128)}, u32[]{:S(2)}) copy-start(s32[1,2,8]{2,1,0:T(2,128)} %param.17) | copy-start | bytes 196
  87.9 11.1 %all-to-all-start.5 = ((bf16[8,32,640]{2,1,0:T(8,128)(2,1)}), bf16[8,32,640]{2,1,0:T(8,128)(2,1)S(1)}, u32[]{:S(2)}, u32[]{:S(2)}) async-start(bf16[8,32,640]{2,1,0:T(8,128)(2,1)} %maximum_bitcast_fusion), calls=%async_computation.5 | async-start | bytes 655360 | tf_op jit(solution)/shard_map/all_to_all | solution.py:19
  99.9 8.8 %all-to-all-start.6 = ((bf16[8,32,256]{2,1,0:T(8,128)(2,1)}), bf16[8,32,256]{2,1,0:T(8,128)(2,1)S(1)}, u32[]{:S(2)}, u32[]{:S(2)}) async-start(bf16[8,32,256]{2,1,0:T(8,128)(2,1)} %broadcast_in_dim.104), calls=%async_computation.6 | async-start | bytes 262144 | tf_op jit(solution)/shard_map/all_to_all | solution.py:19
  112.2 13.1 %all-to-all-start.7 = ((bf16[16,2,896]{2,1,0:T(2,128)(2,1)}), bf16[16,2,896]{2,1,0:T(2,128)(2,1)S(1)}, u32[]{:S(2)}, u32[]{:S(2)}) async-start(bf16[16,2,896]{2,1,0:T(2,128)(2,1)} %bitcast.27), calls=%async_computation.7 | async-start | bytes 114688 | tf_op jit(solution)/shard_map/all_to_all | solution.py:19
